TPU v7x, 32 devices: a whole 2x2x4 slice. The times are simulated.
32 devices in a mesh: slide: 4 (over y, x), seq: 8 (over z, core).
Axes of the slice: x: 2, y: 2, z: 4, core: 2. Of those that a mesh axis runs over, the one named last changes fastest.
Arguments:
- query_tiles: bfloat16 [32768, 768], P(('slide', 'seq')), parts along dimension 0, may hold values from -160 to 160
- key_tiles: bfloat16 [32768, 768], P(('slide', 'seq')), parts along dimension 0, may hold values from -4.04 to 4.04
- value_tiles: bfloat16 [32768, 768], P(('slide', 'seq')), parts along dimension 0, may hold values from -6 to 6
- slide_length: int32 [4], P('slide'), parts along dimension 0, may hold values from 7680 to 8192
Outputs:
- attended: bfloat16 [32768, 768], P(('slide', 'seq')), parts along dimension 0
There are 4 independent parts, one for each index of `slide`. A program takes and returns all parts, laid end to end along the dimension named above; each array names one. Nothing has to cross between parts.
All inputs are finite; a program needn't handle non-finite values.
Results may differ from a plain program's by a relative error of at most 0.0045.
Values may be sent and summed in bfloat16 or wider, within the bound.
A program may use at most 128 MiB of HBM per device.

v0:
```python
import functools
import math

import jax
import jax.numpy as jnp
from jax import lax
from jax.experimental import pallas as pl
from jax.experimental.pallas import tpu as pltpu
from jax.sharding import PartitionSpec as P

HEADS = 12
WIDTH = 768
SEG0 = 512
CLASSES = 16
PAIRS = HEADS // 2
RUN = SEG0 // CLASSES
LANES = 128
MESH = pl.DeviceIdType.MESH
BF16 = jnp.bfloat16
F32 = jnp.float32
EXP_SCALE = 0.125 * math.log2(math.e)
MASK = -1e9


def bitrev(c):
    return (c % 2) * 8 + (c // 2 % 2) * 4 + (c // 4 % 2) * 2 + c // 8 % 2


def rows_at(start, size):
    return pl.ds(pl.multiple_of(start, RUN), size)


def pair_lanes(j, base=0):
    return pl.ds(pl.multiple_of(base + j * LANES, LANES), LANES)


def iota(shape, dim):
    return lax.broadcasted_iota(jnp.int32, shape, dim)


def attend(q, k, v):
    scores = lax.dot_general(q, k, (((1,), (1,)), ((), ())), preferred_element_type=F32)
    peak = jnp.max(scores, axis=1, keepdims=True)
    weights = jnp.exp2((scores - peak) * EXP_SCALE).astype(BF16)
    return jnp.dot(weights, v, preferred_element_type=F32), peak


def merge(acc, peak, acc_b, peak_b):
    top = jnp.maximum(peak, peak_b)
    keep = jnp.exp2((peak - top) * EXP_SCALE)
    add = jnp.exp2((peak_b - top) * EXP_SCALE)
    return acc * keep + acc_b * add, top


def kernel(
    n, len_ref, q_ref, k_ref, v_ref, out_ref,
    qp, kp, vp, r16, r8, r4, bias0, acc_s, peak_s, outp,
    send16, recv16, send8, recv8, send4, recv4, fwd16, fwd8,
):
    shard = q_ref.shape[0]
    segs = shard // SEG0
    chips = n // 2
    me = lax.axis_index("seq")
    chip, core = me // 2, me % 2
    sibling = chip * 2 + 1 - core
    mate_chip = chip + 1 - 2 * (chip % 2)
    mate = mate_chip * 2 + core
    length = len_ref[0]

    barrier = pltpu.get_barrier_semaphore()
    peers = [sibling] + [(chip + step) % chips * 2 + core for step in range(1, chips)]
    for peer in peers:
        pl.semaphore_signal(barrier, inc=1, device_id={"seq": peer}, device_id_type=MESH)

    half = SEG0 // 2
    sub = half // CLASSES
    new = iota((half, half), 0)
    old = iota((half, half), 1)
    shuffle = jnp.where(old == (new % sub) * CLASSES + bitrev(new // sub), 1.0, 0.0).astype(BF16)

    def permute(src, dst):
        def column(step, _):
            lanes = pl.ds(pl.multiple_of(step * 256, 256), 256)
            for t in range(segs):
                for u in range(2):
                    rows = src[pl.ds(t * SEG0 + u * half, half), lanes]
                    moved = jnp.dot(shuffle, rows, preferred_element_type=F32).astype(BF16)
                    for i in range(CLASSES):
                        dst[t, pl.ds(i * RUN + u * sub, sub), lanes] = moved[i * sub:(i + 1) * sub]
            return 0
        lax.fori_loop(0, WIDTH // 256, column, 0)

    permute(k_ref, kp)
    permute(v_ref, vp)

    lane = iota((1, LANES), 1)
    even = jnp.where(lane < 64, 1.0, 0.0).astype(BF16)
    odd = jnp.where(lane < 64, 0.0, 1.0).astype(BF16)
    sides = ((even, odd), (odd, even))

    def gather(j, _):
        for src, base in ((kp, 0), (vp, WIDTH)):
            here = pair_lanes(j)
            there = pair_lanes(j, base)
            for t in range(segs):
                def mixed(shift, keep, size):
                    e = src[t, rows_at(bitrev((2 * j + shift) % keep) * RUN, size), here]
                    o = src[t, rows_at(bitrev((2 * j + 1 + shift) % keep) * RUN, size), here]
                    return e * even + o * odd
                r16[me, pl.ds(t * RUN, RUN), there] = mixed(0, 16, RUN)
                r8[me % 4, pl.ds(t * RUN, RUN), there] = mixed(8, 16, RUN)
                r4[me % 2, pl.ds(t * 2 * RUN, 2 * RUN), there] = mixed(4, 8, 2 * RUN)
        return 0

    lax.fori_loop(0, PAIRS, gather, 0)

    pl.semaphore_wait(barrier, chips)

    def copy(buf, slot, send, recv, peer):
        return pltpu.make_async_remote_copy(
            src_ref=buf.at[slot], dst_ref=buf.at[slot], send_sem=send, recv_sem=recv.at[slot],
            device_id={"seq": peer}, device_id_type=MESH,
        )

    first = []
    for step in range(chips - 1, 0, -1):
        first.append(copy(r16, me, send16.at[step], recv16, (chip + step) % chips * 2 + core))
    first.append(copy(r8, me % 4, send8.at[1], recv8, mate))
    first.append(copy(r16, me, send16.at[0], recv16, sibling))
    first.append(copy(r8, me % 4, send8.at[0], recv8, sibling))
    first.append(copy(r4, me % 2, send4.at[0], recv4, sibling))
    for c in first:
        c.start()

    permute(q_ref, qp)

    row = iota((SEG0, LANES), 0)
    for t in range(segs):
        place = me * shard + t * SEG0 + (row % RUN) * CLASSES + bitrev(row // RUN)
        bias0[t] = jnp.where(place < length, 0.0, MASK).astype(BF16)

    def near(j, _):
        here = pair_lanes(j)
        for side in range(2):
            mine, other = sides[side]
            h = 2 * j + side

            def prep(t, rows):
                k = kp[t, rows, here] * mine + bias0[t, rows, :] * other
                v = vp[t, rows, here] * mine + other
                return k, v

            def query(t, rows):
                return qp[t, rows, here] * mine + other

            for t in range(segs):
                k, v = prep(t, pl.ds(0, SEG0))
                for u in range(2):
                    rows = pl.ds(u * half, half)
                    acc, peak = attend(query(t, rows), k, v)
                    acc_s[h, t, rows, :] = acc
                    peak_s[h, t, rows, :] = jnp.broadcast_to(peak, (half, LANES))
            mid = rows_at((h % 2) * half, half)
            parts = [prep(t, mid) for t in range(segs)]
            k = jnp.concatenate([p[0] for p in parts], axis=0)
            v = jnp.concatenate([p[1] for p in parts], axis=0)
            for t in range(segs):
                acc, peak = attend(query(t, mid), k, v)
                acc, peak = merge(acc_s[h, t, mid, :], peak_s[h, t, mid, :], acc, peak)
                acc_s[h, t, mid, :] = acc
                peak_s[h, t, mid, :] = peak
        return 0

    split = 4
    lax.fori_loop(0, split, near, 0)

    second = []
    for step in range(1, chips):
        source = (chip + chips - step) % chips * 2 + core
        copy(r16, source, send16.at[step], recv16, sibling).wait_recv()
        c = copy(r16, source, fwd16.at[step], recv16, sibling)
        c.start()
        second.append(c)
    copy(r8, mate % 4, send8.at[1], recv8, sibling).wait_recv()
    c = copy(r8, mate % 4, fwd8.at[0], recv8, sibling)
    c.start()
    second.append(c)

    lax.fori_loop(split, PAIRS, near, 0)

    copy(r16, sibling, send16.at[0], recv16, sibling).wait_recv()
    copy(r8, sibling % 4, send8.at[0], recv8, sibling).wait_recv()
    copy(r4, sibling % 2, send4.at[0], recv4, sibling).wait_recv()
    for step in range(1, chips):
        source = (chip + chips - step) % chips * 2 + 1 - core
        copy(r16, source, fwd16.at[step], recv16, sibling).wait_recv()
    far_mate = mate_chip * 2 + 1 - core
    copy(r8, far_mate % 4, fwd8.at[0], recv8, sibling).wait_recv()

    head_lane = 1 - iota((1, LANES), 1) // 64

    def far(j, _):
        here = pair_lanes(j)
        there = pair_lanes(j, WIDTH)
        heads = 2 * j + head_lane

        def bias(slot, size, shift, keep):
            r = iota((size, LANES), 0)
            width = size // segs
            inner = r % width
            place = (
                slot * shard + r // width * SEG0 + inner % RUN * CLASSES
                + inner // RUN * 8 + (heads + shift) % keep
            )
            return jnp.where(place < length, 0.0, MASK).astype(BF16)

        def keys(buf, start, count, size, shift, keep, owner):
            k = buf[pl.ds(start, count), :, here]
            v = buf[pl.ds(start, count), :, there]
            return k, v, bias(owner, size, shift, keep)

        def listed(pieces, mine, other):
            ks, vs = [], []
            for k, v, b in pieces:
                last = k.shape[0] - 1
                ks.append((k[:last] * mine).reshape(-1, LANES))
                ks.append(k[last] * mine + b * other)
                vs.append((v * mine + other).reshape(-1, LANES))
            return jnp.concatenate(ks, axis=0), jnp.concatenate(vs, axis=0)

        two, four = me // 2 * 2, me // 4 * 4
        small = segs * RUN
        lists = (
            (4, (
                keys(r16, two, 2, small, 0, 16, two + 1),
                keys(r8, two % 4, 2, small, 8, 16, two + 1),
                keys(r4, 0, 2, 2 * small, 4, 8, two + 1),
            )),
            (8, (
                keys(r16, four, 4, small, 0, 16, four + 3),
                keys(r8, 0, 4, small, 8, 16, four + 3),
            )),
            (16, (keys(r16, 0, n, small, 0, 16, n - 1),)),
        )
        for side in range(2):
            mine, other = sides[side]
            h = 2 * j + side
            for stride, pieces in lists:
                size = SEG0 // stride
                group = CLASSES // stride
                rows = rows_at(bitrev(h) // group * size, size)
                k, v = listed(pieces, mine, other)
                q = jnp.concatenate([qp[t, rows, here] for t in range(segs)], axis=0)
                acc, peak = attend(q * mine + other, k, v)
                for t in range(segs):
                    part = slice(t * size, (t + 1) * size)
                    acc_t, peak_t = merge(
                        acc_s[h, t, rows, :], peak_s[h, t, rows, :], acc[part], peak[part]
                    )
                    acc_s[h, t, rows, :] = acc_t
                    peak_s[h, t, rows, :] = peak_t
        wide = iota((SEG0, LANES), 1) < 64
        for t in range(segs):
            acc_e, acc_o = acc_s[2 * j, t], acc_s[2 * j + 1, t]
            total = pltpu.roll(jnp.where(wide, acc_o, acc_e), 64, 1)
            outp[t, :, here] = (jnp.where(wide, acc_e, acc_o) / total).astype(BF16)
        return 0

    lax.fori_loop(0, PAIRS, far, 0)

    back = jnp.where(new == (old % sub) * CLASSES + bitrev(old // sub), 1.0, 0.0).astype(BF16)

    def restore(step, _):
        lanes = pl.ds(pl.multiple_of(step * 256, 256), 256)
        for t in range(segs):
            for u in range(2):
                rows = jnp.concatenate(
                    [outp[t, pl.ds(i * RUN + u * sub, sub), lanes] for i in range(CLASSES)], axis=0
                )
                moved = jnp.dot(back, rows, preferred_element_type=F32)
                place = me * shard + t * SEG0 + u * half + iota((half, 256), 0)
                out_ref[pl.ds(t * SEG0 + u * half, half), lanes] = jnp.where(
                    place < length, moved, 0.0
                ).astype(BF16)
        return 0

    lax.fori_loop(0, WIDTH // 256, restore, 0)

    for c in first + second:
        c.wait_send()


def per_device(n, query_tiles, key_tiles, value_tiles, slide_length):
    shard = query_tiles.shape[0]
    segs = shard // SEG0
    chips = n // 2
    small = segs * RUN
    vmem = pl.BlockSpec(memory_space=pltpu.VMEM)
    dma = pltpu.SemaphoreType.DMA
    return pl.pallas_call(
        functools.partial(kernel, n),
        out_shape=jax.ShapeDtypeStruct((shard, WIDTH), BF16),
        in_specs=[pl.BlockSpec(memory_space=pltpu.SMEM), vmem, vmem, vmem],
        out_specs=vmem,
        scratch_shapes=[
            pltpu.VMEM((segs, SEG0, WIDTH), BF16),
            pltpu.VMEM((segs, SEG0, WIDTH), BF16),
            pltpu.VMEM((segs, SEG0, WIDTH), BF16),
            pltpu.VMEM((n, small, 2 * WIDTH), BF16),
            pltpu.VMEM((4, small, 2 * WIDTH), BF16),
            pltpu.VMEM((2, 2 * small, 2 * WIDTH), BF16),
            pltpu.VMEM((segs, SEG0, LANES), BF16),
            pltpu.VMEM((HEADS, segs, SEG0, LANES), F32),
            pltpu.VMEM((HEADS, segs, SEG0, LANES), F32),
            pltpu.VMEM((segs, SEG0, WIDTH), BF16),
            dma((chips,)), dma((n,)), dma((2,)), dma((4,)), dma((1,)), dma((2,)),
            dma((chips,)), dma((1,)),
        ],
        compiler_params=pltpu.CompilerParams(
            collective_id=0, has_side_effects=True, vmem_limit_bytes=56 * 1024 * 1024
        ),
        cost_estimate=pl.CostEstimate(
            flops=256 * shard * HEADS * 1024, bytes_accessed=8 * shard * WIDTH,
            transcendentals=shard * HEADS * 1024,
        ),
    )(slide_length, query_tiles, key_tiles, value_tiles)


def solution(mesh):
    placed = P(("slide", "seq"), None)
    return jax.shard_map(
        functools.partial(per_device, mesh.shape["seq"]),
        mesh=mesh,
        in_specs=(placed, placed, placed, P("slide")),
        out_specs=placed,
        check_vma=False,
    )
```

profile of v0, /device:TPU:0, one launch (start us, length us, event | category | flops | bytes accessed | tf_op | source)
XLA Modules:
  0.0 53.4 jit_solution(4814240609496205207)
XLA Ops:
  0.7 50.0 %shard_map.46 = bf16[1024,768]{1,0:T(8,128)(2,1)} custom-call(s32[1]{0:T(128)S(6)} %copy.6.len_ref, bf16[1024,768]{1,0:T(8,128)(2,1)} %q_ref.1, bf16[1024,768]{1,0:T(8,128)(2,1)} %k_ref.1, bf16[1024,768]{1,0:T(8,128)(2,1)} %v_ref.1), custom_call_target="tpu_custom_call" | custom-call | flops 3221225472 | bytes 6291456 | tf_op jit(solution)/shard_map/pallas_call | solution.py:300
  50.7 2.7 %copy.7 = bf16[1024,768]{1,0:T(8,128)(2,1)} copy(bf16[1024,768]{1,0:T(8,128)(2,1)} %shard_map.46) | data formatting | bytes 3145728
where the time goes:
time: 53.5 us; the launch traced here: 53.4 us
  Pallas kernels  50 us (93%)
  local copies, waits for them, and re-layouts  2.65 us (5%)
  between operations  0.66 us (1%)
    pallas_call x1, Pallas kernels, per_device(): pl.pallas_call(functools.partial(kernel, n), out_shape=jax.ShapeDtypeStru...  50 us
    unnamed x1, local copies, waits for them, and re-layouts  2.65 us

commit v1 on v0

--- a/solution.py
+++ b/solution.py
@@ -38,11 +38,20 @@
     return lax.broadcasted_iota(jnp.int32, shape, dim)
 
 
-def attend(q, k, v):
-    scores = lax.dot_general(q, k, (((1,), (1,)), ((), ())), preferred_element_type=F32)
-    peak = jnp.max(scores, axis=1, keepdims=True)
-    weights = jnp.exp2((scores - peak) * EXP_SCALE).astype(BF16)
-    return jnp.dot(weights, v, preferred_element_type=F32), peak
+def staged(units):
+    held = None
+    for unit in units + [None]:
+        ahead = None
+        if unit is not None:
+            q, k, v, take = unit
+            scores = lax.dot_general(q, k, (((1,), (1,)), ((), ())), preferred_element_type=F32)
+            ahead = (scores, v, take)
+        if held is not None:
+            scores, v, take = held
+            peak = jnp.max(scores, axis=1, keepdims=True)
+            weights = jnp.exp2((scores - peak) * EXP_SCALE).astype(BF16)
+            take(jnp.dot(weights, v, preferred_element_type=F32), peak)
+        held = ahead
 
 
 def merge(acc, peak, acc_b, peak_b):
@@ -141,34 +150,48 @@
 
     def near(j, _):
         here = pair_lanes(j)
+        units = []
         for side in range(2):
             mine, other = sides[side]
             h = 2 * j + side
-
-            def prep(t, rows):
-                k = kp[t, rows, here] * mine + bias0[t, rows, :] * other
-                v = vp[t, rows, here] * mine + other
-                return k, v
+            mid = pl.ds(side * half, half)
+            low = pl.ds((1 - side) * half, half)
+
+            def keys(t, rows):
+                return kp[t, rows, here] * mine + bias0[t, rows, :] * other
+
+            def values(t, rows):
+                return vp[t, rows, here] * mine + other
 
             def query(t, rows):
                 return qp[t, rows, here] * mine + other
 
-            for t in range(segs):
-                k, v = prep(t, pl.ds(0, SEG0))
-                for u in range(2):
-                    rows = pl.ds(u * half, half)
-                    acc, peak = attend(query(t, rows), k, v)
-                    acc_s[h, t, rows, :] = acc
-                    peak_s[h, t, rows, :] = jnp.broadcast_to(peak, (half, LANES))
-            mid = rows_at((h % 2) * half, half)
-            parts = [prep(t, mid) for t in range(segs)]
-            k = jnp.concatenate([p[0] for p in parts], axis=0)
-            v = jnp.concatenate([p[1] for p in parts], axis=0)
-            for t in range(segs):
-                acc, peak = attend(query(t, mid), k, v)
-                acc, peak = merge(acc_s[h, t, mid, :], peak_s[h, t, mid, :], acc, peak)
-                acc_s[h, t, mid, :] = acc
-                peak_s[h, t, mid, :] = peak
+            def keep_low(t, h=h, low=low):
+                def take(acc, peak):
+                    acc_s[h, t, low, :] = acc
+                return take
+
+            def keep_mid(t, h=h, mid=mid):
+                def take(acc, peak):
+                    acc_s[h, t, mid, :] = acc
+                    peak_s[h, t] = jnp.broadcast_to(peak, (half, LANES))
+                return take
+
+            k_all = jnp.concatenate([keys(0, low), keys(0, mid), keys(1, mid), keys(1, low)], axis=0)
+            low0, mid0, mid1, low1 = values(0, low), values(0, mid), values(1, mid), values(1, low)
+            units += [
+                (query(0, low), k_all[:2 * half], jnp.concatenate([low0, mid0], axis=0), keep_low(0)),
+                (
+                    query(0, mid), k_all[:3 * half],
+                    jnp.concatenate([low0, mid0 + mid0, mid1], axis=0), keep_mid(0),
+                ),
+                (
+                    query(1, mid), k_all[half:],
+                    jnp.concatenate([mid0, mid1 + mid1, low1], axis=0), keep_mid(1),
+                ),
+                (query(1, low), k_all[2 * half:], jnp.concatenate([mid1, low1], axis=0), keep_low(1)),
+            ]
+        staged(units)
         return 0
 
     split = 4
@@ -242,23 +265,30 @@
             )),
             (16, (keys(r16, 0, n, small, 0, 16, n - 1),)),
         )
+        units = []
         for side in range(2):
             mine, other = sides[side]
             h = 2 * j + side
             for stride, pieces in lists:
                 size = SEG0 // stride
                 group = CLASSES // stride
-                rows = rows_at(bitrev(h) // group * size, size)
+                start = bitrev(h) // group * size
                 k, v = listed(pieces, mine, other)
-                q = jnp.concatenate([qp[t, rows, here] for t in range(segs)], axis=0)
-                acc, peak = attend(q * mine + other, k, v)
-                for t in range(segs):
-                    part = slice(t * size, (t + 1) * size)
-                    acc_t, peak_t = merge(
-                        acc_s[h, t, rows, :], peak_s[h, t, rows, :], acc[part], peak[part]
-                    )
-                    acc_s[h, t, rows, :] = acc_t
-                    peak_s[h, t, rows, :] = peak_t
+                q = jnp.concatenate([qp[t, rows_at(start, size), here] for t in range(segs)], axis=0)
+
+                def take(acc, peak, h=h, start=start, size=size, side=side):
+                    rows = rows_at(start, size)
+                    inner = rows_at(start - side * half, size)
+                    for t in range(segs):
+                        part = slice(t * size, (t + 1) * size)
+                        acc_t, peak_t = merge(
+                            acc_s[h, t, rows, :], peak_s[h, t, inner, :], acc[part], peak[part]
+                        )
+                        acc_s[h, t, rows, :] = acc_t
+                        peak_s[h, t, inner, :] = peak_t
+
+                units.append((q * mine + other, k, v, take))
+        staged(units)
         wide = iota((SEG0, LANES), 1) < 64
         for t in range(segs):
             acc_e, acc_o = acc_s[2 * j, t], acc_s[2 * j + 1, t]
@@ -311,7 +341,7 @@
             pltpu.VMEM((2, 2 * small, 2 * WIDTH), BF16),
             pltpu.VMEM((segs, SEG0, LANES), BF16),
             pltpu.VMEM((HEADS, segs, SEG0, LANES), F32),
-            pltpu.VMEM((HEADS, segs, SEG0, LANES), F32),
+            pltpu.VMEM((HEADS, segs, SEG0 // 2, LANES), F32),
             pltpu.VMEM((segs, SEG0, WIDTH), BF16),
             dma((chips,)), dma((n,)), dma((2,)), dma((4,)), dma((1,)), dma((2,)),
             dma((chips,)), dma((1,)),

time: 53.5 us -> 45.6 us (0.85)
  Pallas kernels: 50 us -> 42.1 us
    pallas_call x1, Pallas kernels: 50 us -> 42.1 us  [per_device(): pl.pallas_call(functools.partial(kernel, n), out_shape=jax.ShapeDtypeStru...]
where the time goes in v1:
time: 45.6 us; the launch traced here: 45.4 us
  Pallas kernels  42.1 us (92%)
  local copies, waits for them, and re-layouts  2.65 us (6%)
  between operations  0.66 us (1%)
    pallas_call x1, Pallas kernels, per_device(): pl.pallas_call(functools.partial(kernel, n), out_shape=jax.ShapeDtypeStru...  42.1 us
    unnamed x1, local copies, waits for them, and re-layouts  2.65 us

profile of v1, /device:TPU:0, one launch (start us, length us, event | category | flops | bytes accessed | tf_op | source)
XLA Modules:
  0.0 45.4 jit_solution(7495564213908571210)
XLA Ops:
  0.7 42.1 %shard_map.46 = bf16[1024,768]{1,0:T(8,128)(2,1)} custom-call(s32[1]{0:T(128)S(6)} %copy.6.len_ref, bf16[1024,768]{1,0:T(8,128)(2,1)} %q_ref.1, bf16[1024,768]{1,0:T(8,128)(2,1)} %k_ref.1, bf16[1024,768]{1,0:T(8,128)(2,1)} %v_ref.1), custom_call_target="tpu_custom_call" | custom-call | flops 3221225472 | bytes 6291456 | tf_op jit(solution)/shard_map/pallas_call | solution.py:330
  42.8 2.7 %copy.7 = bf16[1024,768]{1,0:T(8,128)(2,1)} copy(bf16[1024,768]{1,0:T(8,128)(2,1)} %shard_map.46) | data formatting | bytes 3145728

commit v2 on v1

--- a/solution.py
+++ b/solution.py
@@ -44,11 +44,12 @@
         ahead = None
         if unit is not None:
             q, k, v, take = unit
-            scores = lax.dot_general(q, k, (((1,), (1,)), ((), ())), preferred_element_type=F32)
+            scores = jnp.dot(q, k, preferred_element_type=F32)
             ahead = (scores, v, take)
         if held is not None:
             scores, v, take = held
-            peak = jnp.max(scores, axis=1, keepdims=True)
+            columns = [scores[:, at:at + LANES] for at in range(0, scores.shape[1], LANES)]
+            peak = jnp.max(functools.reduce(jnp.maximum, columns), axis=1, keepdims=True)
             weights = jnp.exp2((scores - peak) * EXP_SCALE).astype(BF16)
             take(jnp.dot(weights, v, preferred_element_type=F32), peak)
         held = ahead
@@ -143,22 +144,34 @@
 
     permute(q_ref, qp)
 
-    row = iota((SEG0, LANES), 0)
+    def bias_rows(place):
+        fill = jnp.where(place < length, 0.0, MASK)
+        return jnp.broadcast_to(fill, (LANES // 2, fill.shape[1])).astype(BF16)
+
+    def one_head(kt, fill, side):
+        mine = kt[side * 64:side * 64 + 64]
+        return jnp.concatenate([fill, mine] if side else [mine, fill], axis=0)
+
+    column = iota((1, SEG0), 1)
     for t in range(segs):
-        place = me * shard + t * SEG0 + (row % RUN) * CLASSES + bitrev(row // RUN)
-        bias0[t] = jnp.where(place < length, 0.0, MASK).astype(BF16)
+        place = me * shard + t * SEG0 + (column % RUN) * CLASSES + bitrev(column // RUN)
+        bias0[t] = bias_rows(place)
 
     def near(j, _):
         here = pair_lanes(j)
         units = []
+        kt = [jnp.transpose(kp[t, :, here]) for t in range(segs)]
         for side in range(2):
             mine, other = sides[side]
             h = 2 * j + side
             mid = pl.ds(side * half, half)
             low = pl.ds((1 - side) * half, half)
 
-            def keys(t, rows):
-                return kp[t, rows, here] * mine + bias0[t, rows, :] * other
+            full = [one_head(kt[t], bias0[t], side) for t in range(segs)]
+
+            def keys(t, mid_rows):
+                at = half if bool(side) == mid_rows else 0
+                return full[t][:, at:at + half]
 
             def values(t, rows):
                 return vp[t, rows, here] * mine + other
@@ -177,19 +190,21 @@
                     peak_s[h, t] = jnp.broadcast_to(peak, (half, LANES))
                 return take
 
-            k_all = jnp.concatenate([keys(0, low), keys(0, mid), keys(1, mid), keys(1, low)], axis=0)
+            k_all = jnp.concatenate(
+                [keys(0, False), keys(0, True), keys(1, True), keys(1, False)], axis=1
+            )
             low0, mid0, mid1, low1 = values(0, low), values(0, mid), values(1, mid), values(1, low)
             units += [
-                (query(0, low), k_all[:2 * half], jnp.concatenate([low0, mid0], axis=0), keep_low(0)),
+                (query(0, low), k_all[:, :2 * half], jnp.concatenate([low0, mid0], axis=0), keep_low(0)),
                 (
-                    query(0, mid), k_all[:3 * half],
+                    query(0, mid), k_all[:, :3 * half],
                     jnp.concatenate([low0, mid0 + mid0, mid1], axis=0), keep_mid(0),
                 ),
                 (
-                    query(1, mid), k_all[half:],
+                    query(1, mid), k_all[:, half:],
                     jnp.concatenate([mid0, mid1 + mid1, low1], axis=0), keep_mid(1),
                 ),
-                (query(1, low), k_all[2 * half:], jnp.concatenate([mid1, low1], axis=0), keep_low(1)),
+                (query(1, low), k_all[:, 2 * half:], jnp.concatenate([mid1, low1], axis=0), keep_low(1)),
             ]
         staged(units)
         return 0
@@ -220,60 +235,50 @@
     far_mate = mate_chip * 2 + 1 - core
     copy(r8, far_mate % 4, fwd8.at[0], recv8, sibling).wait_recv()
 
-    head_lane = 1 - iota((1, LANES), 1) // 64
-
     def far(j, _):
         here = pair_lanes(j)
         there = pair_lanes(j, WIDTH)
-        heads = 2 * j + head_lane
-
-        def bias(slot, size, shift, keep):
-            r = iota((size, LANES), 0)
+
+        def piece(buf, start, count, shift, keep, owner):
+            size = buf.shape[1]
             width = size // segs
+            r = iota((1, count * size), 1)
             inner = r % width
             place = (
-                slot * shard + r // width * SEG0 + inner % RUN * CLASSES
-                + inner // RUN * 8 + (heads + shift) % keep
+                (owner + r // size) * shard + r % size // width * SEG0
+                + inner % RUN * CLASSES + inner // RUN * 8
             )
-            return jnp.where(place < length, 0.0, MASK).astype(BF16)
-
-        def keys(buf, start, count, size, shift, keep, owner):
-            k = buf[pl.ds(start, count), :, here]
-            v = buf[pl.ds(start, count), :, there]
-            return k, v, bias(owner, size, shift, keep)
-
-        def listed(pieces, mine, other):
-            ks, vs = [], []
-            for k, v, b in pieces:
-                last = k.shape[0] - 1
-                ks.append((k[:last] * mine).reshape(-1, LANES))
-                ks.append(k[last] * mine + b * other)
-                vs.append((v * mine + other).reshape(-1, LANES))
-            return jnp.concatenate(ks, axis=0), jnp.concatenate(vs, axis=0)
+            k = buf[pl.ds(start, count), :, here].reshape(-1, LANES)
+            v = buf[pl.ds(start, count), :, there].reshape(-1, LANES)
+            return k, v, place, shift, keep
+
+        def listed(pieces):
+            k = jnp.concatenate([p[0] for p in pieces], axis=0)
+            v = jnp.concatenate([p[1] for p in pieces], axis=0)
+            return jnp.transpose(k), v, [p[2:] for p in pieces]
 
         two, four = me // 2 * 2, me // 4 * 4
-        small = segs * RUN
         lists = (
-            (4, (
-                keys(r16, two, 2, small, 0, 16, two + 1),
-                keys(r8, two % 4, 2, small, 8, 16, two + 1),
-                keys(r4, 0, 2, 2 * small, 4, 8, two + 1),
-            )),
-            (8, (
-                keys(r16, four, 4, small, 0, 16, four + 3),
-                keys(r8, 0, 4, small, 8, 16, four + 3),
-            )),
-            (16, (keys(r16, 0, n, small, 0, 16, n - 1),)),
+            (4, listed((
+                piece(r16, two, 2, 0, 16, two),
+                piece(r8, two % 4, 2, 8, 16, two),
+                piece(r4, 0, 2, 4, 8, two),
+            ))),
+            (8, listed((piece(r16, four, 4, 0, 16, four), piece(r8, 0, 4, 8, 16, four)))),
+            (16, listed((piece(r16, 0, n, 0, 16, 0),))),
         )
         units = []
         for side in range(2):
             mine, other = sides[side]
             h = 2 * j + side
-            for stride, pieces in lists:
+            for stride, (kt, values, places) in lists:
                 size = SEG0 // stride
                 group = CLASSES // stride
                 start = bitrev(h) // group * size
-                k, v = listed(pieces, mine, other)
+                fill = jnp.concatenate(
+                    [bias_rows(place + (h + shift) % keep) for place, shift, keep in places], axis=1
+                )
+                k, v = one_head(kt, fill, side), values * mine + other
                 q = jnp.concatenate([qp[t, rows_at(start, size), here] for t in range(segs)], axis=0)
 
                 def take(acc, peak, h=h, start=start, size=size, side=side):
@@ -339,7 +344,7 @@
             pltpu.VMEM((n, small, 2 * WIDTH), BF16),
             pltpu.VMEM((4, small, 2 * WIDTH), BF16),
             pltpu.VMEM((2, 2 * small, 2 * WIDTH), BF16),
-            pltpu.VMEM((segs, SEG0, LANES), BF16),
+            pltpu.VMEM((segs, LANES // 2, SEG0), BF16),
             pltpu.VMEM((HEADS, segs, SEG0, LANES), F32),
             pltpu.VMEM((HEADS, segs, SEG0 // 2, LANES), F32),
             pltpu.VMEM((segs, SEG0, WIDTH), BF16),

time: 45.6 us -> 45.3 us (level)
  no operation moved by 1% of the time
where the time goes in v2:
time: 45.3 us; the launch traced here: 45.1 us
  Pallas kernels  41.8 us (92%)
  local copies, waits for them, and re-layouts  2.65 us (6%)
  between operations  0.66 us (1%)
    pallas_call x1, Pallas kernels, per_device(): pl.pallas_call(functools.partial(kernel, n), out_shape=jax.ShapeDtypeStru...  41.8 us
    unnamed x1, local copies, waits for them, and re-layouts  2.65 us

profile of v2, /device:TPU:0, one launch (start us, length us, event | category | flops | bytes accessed | tf_op | source)
XLA Modules:
  0.0 45.1 jit_solution(10132188866904084076)
XLA Ops:
  0.7 41.8 %shard_map.46 = bf16[1024,768]{1,0:T(8,128)(2,1)} custom-call(s32[1]{0:T(128)S(6)} %copy.6.len_ref, bf16[1024,768]{1,0:T(8,128)(2,1)} %q_ref.1, bf16[1024,768]{1,0:T(8,128)(2,1)} %k_ref.1, bf16[1024,768]{1,0:T(8,128)(2,1)} %v_ref.1), custom_call_target="tpu_custom_call" | custom-call | flops 3221225472 | bytes 6291456 | tf_op jit(solution)/shard_map/pallas_call | solution.py:335
  42.5 2.7 %copy.7 = bf16[1024,768]{1,0:T(8,128)(2,1)} copy(bf16[1024,768]{1,0:T(8,128)(2,1)} %shard_map.46) | data formatting | bytes 3145728

commit v3 on v2

--- a/solution.py
+++ b/solution.py
@@ -23,7 +23,11 @@
 
 
 def bitrev(c):
-    return (c % 2) * 8 + (c // 2 % 2) * 4 + (c // 4 % 2) * 2 + c // 8 % 2
+    return ((c & 1) << 3) + ((c & 2) << 1) + ((c & 4) >> 1) + ((c & 8) >> 3)
+
+
+def home(j, side):
+    return 8 * side + lax.rem(j, 2) * 4 + lax.rem(lax.div(j, 2), 2) * 2 + lax.div(j, 4)
 
 
 def rows_at(start, size):
@@ -86,7 +90,7 @@
     sub = half // CLASSES
     new = iota((half, half), 0)
     old = iota((half, half), 1)
-    shuffle = jnp.where(old == (new % sub) * CLASSES + bitrev(new // sub), 1.0, 0.0).astype(BF16)
+    shuffle = jnp.where(old == ((new & (sub - 1)) << 4) + bitrev(new >> 4), 1.0, 0.0).astype(BF16)
 
     def permute(src, dst):
         def column(step, _):
@@ -113,13 +117,13 @@
             here = pair_lanes(j)
             there = pair_lanes(j, base)
             for t in range(segs):
-                def mixed(shift, keep, size):
-                    e = src[t, rows_at(bitrev((2 * j + shift) % keep) * RUN, size), here]
-                    o = src[t, rows_at(bitrev((2 * j + 1 + shift) % keep) * RUN, size), here]
+                def mixed(turn, size):
+                    e = src[t, rows_at(turn(home(j, 0)) * RUN, size), here]
+                    o = src[t, rows_at(turn(home(j, 1)) * RUN, size), here]
                     return e * even + o * odd
-                r16[me, pl.ds(t * RUN, RUN), there] = mixed(0, 16, RUN)
-                r8[me % 4, pl.ds(t * RUN, RUN), there] = mixed(8, 16, RUN)
-                r4[me % 2, pl.ds(t * 2 * RUN, 2 * RUN), there] = mixed(4, 8, 2 * RUN)
+                r16[me, pl.ds(t * RUN, RUN), there] = mixed(lambda c: c, RUN)
+                r8[me % 4, pl.ds(t * RUN, RUN), there] = mixed(lambda c: c + 1 - 2 * lax.rem(c, 2), RUN)
+                r4[me % 2, pl.ds(t * 2 * RUN, 2 * RUN), there] = mixed(lambda c: lax.div(c, 4) * 4 + 2 - lax.div(lax.rem(c, 4), 2) * 2, 2 * RUN)
         return 0
 
     lax.fori_loop(0, PAIRS, gather, 0)
@@ -154,7 +158,7 @@
 
     column = iota((1, SEG0), 1)
     for t in range(segs):
-        place = me * shard + t * SEG0 + (column % RUN) * CLASSES + bitrev(column // RUN)
+        place = me * shard + t * SEG0 + ((column & (RUN - 1)) << 4) + bitrev(column >> 5)
         bias0[t] = bias_rows(place)
 
     def near(j, _):
@@ -209,8 +213,7 @@
         staged(units)
         return 0
 
-    split = 4
-    lax.fori_loop(0, split, near, 0)
+    lax.fori_loop(0, PAIRS, near, 0)
 
     second = []
     for step in range(1, chips):
@@ -224,30 +227,23 @@
     c.start()
     second.append(c)
 
-    lax.fori_loop(split, PAIRS, near, 0)
-
     copy(r16, sibling, send16.at[0], recv16, sibling).wait_recv()
     copy(r8, sibling % 4, send8.at[0], recv8, sibling).wait_recv()
     copy(r4, sibling % 2, send4.at[0], recv4, sibling).wait_recv()
-    for step in range(1, chips):
-        source = (chip + chips - step) % chips * 2 + 1 - core
-        copy(r16, source, fwd16.at[step], recv16, sibling).wait_recv()
-    far_mate = mate_chip * 2 + 1 - core
-    copy(r8, far_mate % 4, fwd8.at[0], recv8, sibling).wait_recv()
-
-    def far(j, _):
+    def far(strides, j, _):
         here = pair_lanes(j)
         there = pair_lanes(j, WIDTH)
 
         def piece(buf, start, count, shift, keep, owner):
             size = buf.shape[1]
-            width = size // segs
+            bits = size.bit_length() - 1
             r = iota((1, count * size), 1)
-            inner = r % width
             place = (
-                (owner + r // size) * shard + r % size // width * SEG0
-                + inner % RUN * CLASSES + inner // RUN * 8
+                (owner + (r >> bits)) * shard + ((r >> (bits - 1)) & 1) * SEG0
+                + ((r & (RUN - 1)) << 4)
             )
+            if size > segs * RUN:
+                place = place + ((r >> 5) & 1) * 8
             k = buf[pl.ds(start, count), :, here].reshape(-1, LANES)
             v = buf[pl.ds(start, count), :, there].reshape(-1, LANES)
             return k, v, place, shift, keep
@@ -258,15 +254,19 @@
             return jnp.transpose(k), v, [p[2:] for p in pieces]
 
         two, four = me // 2 * 2, me // 4 * 4
-        lists = (
-            (4, listed((
+        lists = []
+        if 4 in strides:
+            lists.append((4, listed((
                 piece(r16, two, 2, 0, 16, two),
                 piece(r8, two % 4, 2, 8, 16, two),
                 piece(r4, 0, 2, 4, 8, two),
-            ))),
-            (8, listed((piece(r16, four, 4, 0, 16, four), piece(r8, 0, 4, 8, 16, four)))),
-            (16, listed((piece(r16, 0, n, 0, 16, 0),))),
-        )
+            ))))
+        if 8 in strides:
+            lists.append((8, listed((
+                piece(r16, four, 4, 0, 16, four), piece(r8, 0, 4, 8, 16, four),
+            ))))
+        if 16 in strides:
+            lists.append((16, listed((piece(r16, 0, n, 0, 16, 0),))))
         units = []
         for side in range(2):
             mine, other = sides[side]
@@ -274,9 +274,9 @@
             for stride, (kt, values, places) in lists:
                 size = SEG0 // stride
                 group = CLASSES // stride
-                start = bitrev(h) // group * size
+                start = lax.div(home(j, side), group) * size
                 fill = jnp.concatenate(
-                    [bias_rows(place + (h + shift) % keep) for place, shift, keep in places], axis=1
+                    [bias_rows(place + ((h + shift) & (keep - 1))) for place, shift, keep in places], axis=1
                 )
                 k, v = one_head(kt, fill, side), values * mine + other
                 q = jnp.concatenate([qp[t, rows_at(start, size), here] for t in range(segs)], axis=0)
@@ -294,6 +294,8 @@
 
                 units.append((q * mine + other, k, v, take))
         staged(units)
+        if 16 not in strides:
+            return 0
         wide = iota((SEG0, LANES), 1) < 64
         for t in range(segs):
             acc_e, acc_o = acc_s[2 * j, t], acc_s[2 * j + 1, t]
@@ -301,9 +303,17 @@
             outp[t, :, here] = (jnp.where(wide, acc_e, acc_o) / total).astype(BF16)
         return 0
 
-    lax.fori_loop(0, PAIRS, far, 0)
-
-    back = jnp.where(new == (old % sub) * CLASSES + bitrev(old // sub), 1.0, 0.0).astype(BF16)
+    lax.fori_loop(0, PAIRS, functools.partial(far, (4,)), 0)
+
+    for step in range(1, chips):
+        source = (chip + chips - step) % chips * 2 + 1 - core
+        copy(r16, source, fwd16.at[step], recv16, sibling).wait_recv()
+    far_mate = mate_chip * 2 + 1 - core
+    copy(r8, far_mate % 4, fwd8.at[0], recv8, sibling).wait_recv()
+
+    lax.fori_loop(0, PAIRS, functools.partial(far, (8, 16)), 0)
+
+    back = jnp.where(new == ((old & (sub - 1)) << 4) + bitrev(old >> 4), 1.0, 0.0).astype(BF16)
 
     def restore(step, _):
         lanes = pl.ds(pl.multiple_of(step * 256, 256), 256)

time: 45.3 us -> 42.2 us (0.932)
  Pallas kernels: 41.8 us -> 38.8 us
    pallas_call x1, Pallas kernels: 41.8 us -> 38.8 us  [per_device(): pl.pallas_call(functools.partial(kernel, n), out_shape=jax.ShapeDtypeStru...]
where the time goes in v3:
time: 42.2 us; the launch traced here: 42.1 us
  Pallas kernels  38.8 us (92%)
  local copies, waits for them, and re-layouts  2.65 us (6%)
  between operations  0.66 us (2%)
    pallas_call x1, Pallas kernels, per_device(): pl.pallas_call(functools.partial(kernel, n), out_shape=jax.ShapeDtypeStru...  38.8 us
    unnamed x1, local copies, waits for them, and re-layouts  2.65 us

profile of v3, /device:TPU:0, one launch (start us, length us, event | category | flops | bytes accessed | tf_op | source)
XLA Modules:
  0.0 42.1 jit_solution(13652383173963087166)
XLA Ops:
  0.7 38.8 %shard_map.46 = bf16[1024,768]{1,0:T(8,128)(2,1)} custom-call(s32[1]{0:T(128)S(6)} %copy.6.len_ref, bf16[1024,768]{1,0:T(8,128)(2,1)} %q_ref.1, bf16[1024,768]{1,0:T(8,128)(2,1)} %k_ref.1, bf16[1024,768]{1,0:T(8,128)(2,1)} %v_ref.1), custom_call_target="tpu_custom_call" | custom-call | flops 3221225472 | bytes 6291456 | tf_op jit(solution)/shard_map/pallas_call | solution.py:345
  39.4 2.7 %copy.7 = bf16[1024,768]{1,0:T(8,128)(2,1)} copy(bf16[1024,768]{1,0:T(8,128)(2,1)} %shard_map.46) | data formatting | bytes 3145728

commit v4 on v3

--- a/solution.py
+++ b/solution.py
@@ -43,20 +43,17 @@
 
 
 def staged(units):
-    held = None
-    for unit in units + [None]:
-        ahead = None
+    held = []
+    for unit in units + [None, None]:
         if unit is not None:
             q, k, v, take = unit
-            scores = jnp.dot(q, k, preferred_element_type=F32)
-            ahead = (scores, v, take)
-        if held is not None:
-            scores, v, take = held
+            held.append((jnp.dot(q, k, preferred_element_type=F32), v, take))
+        if len(held) > 2 or unit is None and held:
+            scores, v, take = held.pop(0)
             columns = [scores[:, at:at + LANES] for at in range(0, scores.shape[1], LANES)]
             peak = jnp.max(functools.reduce(jnp.maximum, columns), axis=1, keepdims=True)
             weights = jnp.exp2((scores - peak) * EXP_SCALE).astype(BF16)
             take(jnp.dot(weights, v, preferred_element_type=F32), peak)
-        held = ahead
 
 
 def merge(acc, peak, acc_b, peak_b):
@@ -68,7 +65,7 @@
 
 def kernel(
     n, len_ref, q_ref, k_ref, v_ref, out_ref,
-    qp, kp, vp, r16, r8, r4, bias0, acc_s, peak_s, outp,
+    qp, kp, vp, r16, r8, r4, bias0, acc_s, peak_s,
     send16, recv16, send8, recv8, send4, recv4, fwd16, fwd8,
 ):
     shard = q_ref.shape[0]
@@ -161,7 +158,7 @@
         place = me * shard + t * SEG0 + ((column & (RUN - 1)) << 4) + bitrev(column >> 5)
         bias0[t] = bias_rows(place)
 
-    def near(j, _):
+    def near(j):
         here = pair_lanes(j)
         units = []
         kt = [jnp.transpose(kp[t, :, here]) for t in range(segs)]
@@ -210,10 +207,13 @@
                 ),
                 (query(1, low), k_all[:, 2 * half:], jnp.concatenate([mid1, low1], axis=0), keep_low(1)),
             ]
-        staged(units)
+        return units
+
+    def near_step(step, _):
+        staged(near(2 * step) + near(2 * step + 1))
         return 0
 
-    lax.fori_loop(0, PAIRS, near, 0)
+    lax.fori_loop(0, PAIRS // 2, near_step, 0)
 
     second = []
     for step in range(1, chips):
@@ -230,7 +230,7 @@
     copy(r16, sibling, send16.at[0], recv16, sibling).wait_recv()
     copy(r8, sibling % 4, send8.at[0], recv8, sibling).wait_recv()
     copy(r4, sibling % 2, send4.at[0], recv4, sibling).wait_recv()
-    def far(strides, j, _):
+    def far(strides, j):
         here = pair_lanes(j)
         there = pair_lanes(j, WIDTH)
 
@@ -293,17 +293,28 @@
                         peak_s[h, t, inner, :] = peak_t
 
                 units.append((q * mine + other, k, v, take))
-        staged(units)
-        if 16 not in strides:
-            return 0
+        return units
+
+    def finish(j):
+        here = pair_lanes(j)
         wide = iota((SEG0, LANES), 1) < 64
         for t in range(segs):
             acc_e, acc_o = acc_s[2 * j, t], acc_s[2 * j + 1, t]
             total = pltpu.roll(jnp.where(wide, acc_o, acc_e), 64, 1)
-            outp[t, :, here] = (jnp.where(wide, acc_e, acc_o) / total).astype(BF16)
+            done = (jnp.where(wide, acc_e, acc_o) / total).astype(BF16)
+            for u in range(2):
+                for i in range(CLASSES):
+                    at = i * RUN + u * sub
+                    out_ref[pl.ds(t * SEG0 + u * half + i * sub, sub), here] = done[at:at + sub]
+
+    def far_step(strides, step, _):
+        staged(far(strides, 2 * step) + far(strides, 2 * step + 1))
+        if 16 in strides:
+            finish(2 * step)
+            finish(2 * step + 1)
         return 0
 
-    lax.fori_loop(0, PAIRS, functools.partial(far, (4,)), 0)
+    lax.fori_loop(0, PAIRS // 2, functools.partial(far_step, (4,)), 0)
 
     for step in range(1, chips):
         source = (chip + chips - step) % chips * 2 + 1 - core
@@ -311,28 +322,22 @@
     far_mate = mate_chip * 2 + 1 - core
     copy(r8, far_mate % 4, fwd8.at[0], recv8, sibling).wait_recv()
 
-    lax.fori_loop(0, PAIRS, functools.partial(far, (8, 16)), 0)
-
-    back = jnp.where(new == ((old & (sub - 1)) << 4) + bitrev(old >> 4), 1.0, 0.0).astype(BF16)
-
-    def restore(step, _):
-        lanes = pl.ds(pl.multiple_of(step * 256, 256), 256)
-        for t in range(segs):
-            for u in range(2):
-                rows = jnp.concatenate(
-                    [outp[t, pl.ds(i * RUN + u * sub, sub), lanes] for i in range(CLASSES)], axis=0
-                )
-                moved = jnp.dot(back, rows, preferred_element_type=F32)
-                place = me * shard + t * SEG0 + u * half + iota((half, 256), 0)
-                out_ref[pl.ds(t * SEG0 + u * half, half), lanes] = jnp.where(
-                    place < length, moved, 0.0
-                ).astype(BF16)
-        return 0
-
-    lax.fori_loop(0, WIDTH // 256, restore, 0)
+    lax.fori_loop(0, PAIRS // 2, functools.partial(far_step, (8, 16)), 0)
 
     for c in first + second:
         c.wait_send()
+
+
+def restore(len_ref, rows_ref, out_ref):
+    half, width = rows_ref.shape
+    sub = half // CLASSES
+    new = iota((half, half), 0)
+    old = iota((half, half), 1)
+    back = jnp.where(new == ((old & (sub - 1)) << 4) + bitrev(old >> 4), 1.0, 0.0).astype(BF16)
+    first = (lax.axis_index("seq") * pl.num_programs(0) + pl.program_id(0)) * half
+    valid = first + iota((half, 1), 0) < len_ref[0]
+    moved = jnp.dot(back, rows_ref[...], preferred_element_type=F32)
+    out_ref[...] = jnp.where(valid, moved, 0.0).astype(BF16)
 
 
 def per_device(n, query_tiles, key_tiles, value_tiles, slide_length):
@@ -342,7 +347,7 @@
     small = segs * RUN
     vmem = pl.BlockSpec(memory_space=pltpu.VMEM)
     dma = pltpu.SemaphoreType.DMA
-    return pl.pallas_call(
+    shuffled = pl.pallas_call(
         functools.partial(kernel, n),
         out_shape=jax.ShapeDtypeStruct((shard, WIDTH), BF16),
         in_specs=[pl.BlockSpec(memory_space=pltpu.SMEM), vmem, vmem, vmem],
@@ -357,7 +362,6 @@
             pltpu.VMEM((segs, LANES // 2, SEG0), BF16),
             pltpu.VMEM((HEADS, segs, SEG0, LANES), F32),
             pltpu.VMEM((HEADS, segs, SEG0 // 2, LANES), F32),
-            pltpu.VMEM((segs, SEG0, WIDTH), BF16),
             dma((chips,)), dma((n,)), dma((2,)), dma((4,)), dma((1,)), dma((2,)),
             dma((chips,)), dma((1,)),
         ],
@@ -369,6 +373,14 @@
             transcendentals=shard * HEADS * 1024,
         ),
     )(slide_length, query_tiles, key_tiles, value_tiles)
+    block = pl.BlockSpec((SEG0 // 2, WIDTH), lambda i: (i, 0))
+    return pl.pallas_call(
+        restore,
+        grid=(shard // (SEG0 // 2),),
+        out_shape=jax.ShapeDtypeStruct((shard, WIDTH), BF16),
+        in_specs=[pl.BlockSpec(memory_space=pltpu.SMEM), block],
+        out_specs=block,
+    )(slide_length, shuffled)
 
 
 def solution(mesh):

time: 42.2 us -> 40.4 us (0.957)
  local copies, waits for them, and re-layouts: 2.65 us -> 0 us
  Pallas kernels: 38.8 us -> 39.5 us
    pallas_call x0 -> x1, Pallas kernels: none -> 4.06 us  [per_device(): pl.pallas_call(restore, grid=(shard // (SEG0 // 2),), out_shape=jax.Shape...]
    pallas_call x1, Pallas kernels: 38.8 us -> 35.5 us  [per_device(): pl.pallas_call(functools.partial(kernel, n), out_shape=jax.ShapeDtypeStru...]
    unnamed x1 -> x0, local copies, waits for them, and re-layouts: 2.65 us -> none
where the time goes in v4:
time: 40.4 us; the launch traced here: 40.2 us
  Pallas kernels  39.5 us (98%)
  between operations  0.66 us (2%)
    pallas_call x1, Pallas kernels, per_device(): pl.pallas_call(functools.partial(kernel, n), out_shape=jax.ShapeDtypeStru...  35.5 us
    pallas_call x1, Pallas kernels, per_device(): pl.pallas_call(restore, grid=(shard // (SEG0 // 2),), out_shape=jax.Shape...  4.06 us

profile of v4, /device:TPU:0, one launch (start us, length us, event | category | flops | bytes accessed | tf_op | source)
XLA Modules:
  0.0 40.2 jit_solution(13247349183243159094)
XLA Ops:
  0.7 35.5 %shard_map.46.rows_ref = bf16[1024,768]{1,0:T(8,128)(2,1)} custom-call(s32[1]{0:T(128)S(6)} %copy.5.len_ref, bf16[1024,768]{1,0:T(8,128)(2,1)} %q_ref.1, bf16[1024,768]{1,0:T(8,128)(2,1)} %k_ref.1, bf16[1024,768]{1,0:T(8,128)(2,1)} %v_ref.1), custom_call_target="tpu_custom_call" | custom-call | flops 3221225472 | bytes 6291456 | tf_op jit(solution)/shard_map/pallas_call | solution.py:350
  36.1 4.1 %shard_map.47 = bf16[1024,768]{1,0:T(8,128)(2,1)} custom-call(s32[1]{0:T(128)S(6)} %copy.5.len_ref, bf16[1024,768]{1,0:T(8,128)(2,1)} %shard_map.46.rows_ref), custom_call_target="tpu_custom_call" | custom-call | tf_op jit(solution)/shard_map/pallas_call | solution.py:377

commit v5 on v4

--- a/solution.py
+++ b/solution.py
@@ -42,18 +42,26 @@
     return lax.broadcasted_iota(jnp.int32, shape, dim)
 
 
+def dot(a, b):
+    return jnp.dot(a, b, preferred_element_type=F32)
+
+
+def peak_of(*blocks):
+    columns = [x[:, at:at + LANES] for x in blocks for at in range(0, x.shape[1], LANES)]
+    return jnp.max(functools.reduce(jnp.maximum, columns), axis=1, keepdims=True)
+
+
+def weigh(scores, peak):
+    return jnp.exp2((scores - peak) * EXP_SCALE).astype(BF16)
+
+
 def staged(units):
-    held = []
-    for unit in units + [None, None]:
-        if unit is not None:
-            q, k, v, take = unit
-            held.append((jnp.dot(q, k, preferred_element_type=F32), v, take))
-        if len(held) > 2 or unit is None and held:
-            scores, v, take = held.pop(0)
-            columns = [scores[:, at:at + LANES] for at in range(0, scores.shape[1], LANES)]
-            peak = jnp.max(functools.reduce(jnp.maximum, columns), axis=1, keepdims=True)
-            weights = jnp.exp2((scores - peak) * EXP_SCALE).astype(BF16)
-            take(jnp.dot(weights, v, preferred_element_type=F32), peak)
+    held = None
+    for unit in units + [None]:
+        ahead = unit and (unit[0](), unit[1])
+        if held is not None:
+            held[1](*held[0])
+        held = ahead
 
 
 def merge(acc, peak, acc_b, peak_b):
@@ -149,9 +157,18 @@
         fill = jnp.where(place < length, 0.0, MASK)
         return jnp.broadcast_to(fill, (LANES // 2, fill.shape[1])).astype(BF16)
 
-    def one_head(kt, fill, side):
-        mine = kt[side * 64:side * 64 + 64]
-        return jnp.concatenate([fill, mine] if side else [mine, fill], axis=0)
+    wide = iota((1, LANES), 1) < LANES // 2
+
+    def query(q, side):
+        mine = sides[side][0]
+        return jnp.concatenate([q * mine, jnp.zeros_like(q) + mine], axis=1)
+
+    def with_ones(v):
+        return jnp.concatenate([v, jnp.ones_like(v)], axis=1)
+
+    def own_half(acc, side):
+        sums, totals = acc[:, :LANES], acc[:, LANES:]
+        return jnp.where(wide, totals, sums) if side else jnp.where(wide, sums, totals)
 
     column = iota((1, SEG0), 1)
     for t in range(segs):
@@ -160,54 +177,58 @@
 
     def near(j):
         here = pair_lanes(j)
-        units = []
-        kt = [jnp.transpose(kp[t, :, here]) for t in range(segs)]
-        for side in range(2):
-            mine, other = sides[side]
-            h = 2 * j + side
-            mid = pl.ds(side * half, half)
-            low = pl.ds((1 - side) * half, half)
-
-            full = [one_head(kt[t], bias0[t], side) for t in range(segs)]
-
-            def keys(t, mid_rows):
-                at = half if bool(side) == mid_rows else 0
-                return full[t][:, at:at + half]
-
-            def values(t, rows):
-                return vp[t, rows, here] * mine + other
-
-            def query(t, rows):
-                return qp[t, rows, here] * mine + other
-
-            def keep_low(t, h=h, low=low):
-                def take(acc, peak):
-                    acc_s[h, t, low, :] = acc
-                return take
-
-            def keep_mid(t, h=h, mid=mid):
-                def take(acc, peak):
-                    acc_s[h, t, mid, :] = acc
-                    peak_s[h, t] = jnp.broadcast_to(peak, (half, LANES))
-                return take
-
-            k_all = jnp.concatenate(
-                [keys(0, False), keys(0, True), keys(1, True), keys(1, False)], axis=1
-            )
-            low0, mid0, mid1, low1 = values(0, low), values(0, mid), values(1, mid), values(1, low)
-            units += [
-                (query(0, low), k_all[:, :2 * half], jnp.concatenate([low0, mid0], axis=0), keep_low(0)),
-                (
-                    query(0, mid), k_all[:, :3 * half],
-                    jnp.concatenate([low0, mid0 + mid0, mid1], axis=0), keep_mid(0),
-                ),
-                (
-                    query(1, mid), k_all[:, half:],
-                    jnp.concatenate([mid0, mid1 + mid1, low1], axis=0), keep_mid(1),
-                ),
-                (query(1, low), k_all[:, 2 * half:], jnp.concatenate([mid1, low1], axis=0), keep_low(1)),
-            ]
-        return units
+        keys = [
+            jnp.concatenate([jnp.transpose(kp[t, :, here]), bias0[t], bias0[t]], axis=0)
+            for t in range(segs)
+        ]
+        values = [with_ones(vp[t, :, here]) for t in range(segs)]
+
+        def unit(t):
+            far_t = 1 - t
+
+            def start():
+                q = [query(qp[t, :, here], side) for side in range(2)]
+                own = dot(jnp.concatenate(q, axis=0), keys[t])
+                cross = []
+                for side in range(2):
+                    mid = slice(side * half, side * half + half)
+                    cross.append(dot(q[side][mid], keys[far_t][:, mid]))
+                return own, cross
+
+            def take(own, cross):
+                rows = []
+                extra = []
+                for side in range(2):
+                    h = 2 * j + side
+                    for block in range(2):
+                        at = (2 * side + block) * half
+                        scores = own[at:at + half]
+                        if block != side:
+                            rows.append(weigh(scores, peak_of(scores)))
+                            continue
+                        peak = peak_of(scores, cross[side])
+                        weights = weigh(scores, peak)
+                        left, right = weights[:, :half], weights[:, half:]
+                        if side:
+                            right = right + right
+                        else:
+                            left = left + left
+                        rows.append(jnp.concatenate([left, right], axis=1))
+                        mid = slice(side * half, side * half + half)
+                        extra.append(dot(weigh(cross[side], peak), values[far_t][mid]))
+                        peak_s[h, t] = jnp.broadcast_to(peak, (half, LANES))
+                acc = dot(jnp.concatenate(rows, axis=0), values[t])
+                for side in range(2):
+                    for block in range(2):
+                        at = (2 * side + block) * half
+                        part = acc[at:at + half]
+                        if block == side:
+                            part = part + extra[side]
+                        acc_s[2 * j + side, t, pl.ds(block * half, half), :] = own_half(part, side)
+
+            return start, take
+
+        return [unit(t) for t in range(segs)]
 
     def near_step(step, _):
         staged(near(2 * step) + near(2 * step + 1))
@@ -267,37 +288,51 @@
             ))))
         if 16 in strides:
             lists.append((16, listed((piece(r16, 0, n, 0, 16, 0),))))
-        units = []
-        for side in range(2):
-            mine, other = sides[side]
-            h = 2 * j + side
-            for stride, (kt, values, places) in lists:
-                size = SEG0 // stride
-                group = CLASSES // stride
-                start = lax.div(home(j, side), group) * size
-                fill = jnp.concatenate(
-                    [bias_rows(place + ((h + shift) & (keep - 1))) for place, shift, keep in places], axis=1
-                )
-                k, v = one_head(kt, fill, side), values * mine + other
-                q = jnp.concatenate([qp[t, rows_at(start, size), here] for t in range(segs)], axis=0)
-
-                def take(acc, peak, h=h, start=start, size=size, side=side):
-                    rows = rows_at(start, size)
-                    inner = rows_at(start - side * half, size)
+        def unit(stride, kt, v, places):
+            size = SEG0 // stride
+            group = CLASSES // stride
+            count = segs * size
+            starts = [lax.div(home(j, side), group) * size for side in range(2)]
+
+            def start():
+                fills = [
+                    jnp.concatenate(
+                        [
+                            bias_rows(place + ((2 * j + side + shift) & (keep - 1)))
+                            for place, shift, keep in places
+                        ],
+                        axis=1,
+                    )
+                    for side in range(2)
+                ]
+                q = [
+                    query(qp[t, rows_at(starts[side], size), here], side)
+                    for side in range(2) for t in range(segs)
+                ]
+                return (dot(jnp.concatenate(q, axis=0), jnp.concatenate([kt] + fills, axis=0)),)
+
+            def take(scores):
+                peak = peak_of(scores)
+                acc = dot(weigh(scores, peak), with_ones(v))
+                for side in range(2):
+                    h = 2 * j + side
+                    rows = rows_at(starts[side], size)
+                    inner = rows_at(starts[side] - side * half, size)
                     for t in range(segs):
-                        part = slice(t * size, (t + 1) * size)
+                        at = side * count + t * size
                         acc_t, peak_t = merge(
-                            acc_s[h, t, rows, :], peak_s[h, t, inner, :], acc[part], peak[part]
+                            acc_s[h, t, rows, :], peak_s[h, t, inner, :],
+                            own_half(acc[at:at + size], side), peak[at:at + size],
                         )
                         acc_s[h, t, rows, :] = acc_t
                         peak_s[h, t, inner, :] = peak_t
 
-                units.append((q * mine + other, k, v, take))
-        return units
+            return start, take
+
+        return [unit(stride, *rest) for stride, rest in lists]
 
     def finish(j):
         here = pair_lanes(j)
-        wide = iota((SEG0, LANES), 1) < 64
         for t in range(segs):
             acc_e, acc_o = acc_s[2 * j, t], acc_s[2 * j + 1, t]
             total = pltpu.roll(jnp.where(wide, acc_o, acc_e), 64, 1)

time: 40.4 us -> 39.8 us (0.985)
  Pallas kernels: 39.5 us -> 38.9 us
    pallas_call x1, Pallas kernels: 35.5 us -> 34.9 us  [per_device(): pl.pallas_call(functools.partial(kernel, n), out_shape=jax.ShapeDtypeStru...]
where the time goes in v5:
time: 39.8 us; the launch traced here: 39.6 us
  Pallas kernels  38.9 us (98%)
  between operations  0.66 us (2%)
    pallas_call x1, Pallas kernels, per_device(): pl.pallas_call(functools.partial(kernel, n), out_shape=jax.ShapeDtypeStru...  34.9 us
    pallas_call x1, Pallas kernels, per_device(): pl.pallas_call(restore, grid=(shard // (SEG0 // 2),), out_shape=jax.Shape...  4.06 us

profile of v5, /device:TPU:0, one launch (start us, length us, event | category | flops | bytes accessed | tf_op | source)
XLA Modules:
  0.0 39.6 jit_solution(787998248004432215)
XLA Ops:
  0.7 34.9 %shard_map.46.rows_ref = bf16[1024,768]{1,0:T(8,128)(2,1)} custom-call(s32[1]{0:T(128)S(6)} %copy.5.len_ref, bf16[1024,768]{1,0:T(8,128)(2,1)} %q_ref.1, bf16[1024,768]{1,0:T(8,128)(2,1)} %k_ref.1, bf16[1024,768]{1,0:T(8,128)(2,1)} %v_ref.1), custom_call_target="tpu_custom_call" | custom-call | flops 3221225472 | bytes 6291456 | tf_op jit(solution)/shard_map/pallas_call | solution.py:385
  35.5 4.1 %shard_map.47 = bf16[1024,768]{1,0:T(8,128)(2,1)} custom-call(s32[1]{0:T(128)S(6)} %copy.5.len_ref, bf16[1024,768]{1,0:T(8,128)(2,1)} %shard_map.46.rows_ref), custom_call_target="tpu_custom_call" | custom-call | tf_op jit(solution)/shard_map/pallas_call | solution.py:412

commit v6 on v5

--- a/solution.py
+++ b/solution.py
@@ -72,10 +72,16 @@
 
 
 def kernel(
-    n, len_ref, q_ref, k_ref, v_ref, out_ref,
-    qp, kp, vp, r16, r8, r4, bias0, acc_s, peak_s,
+    n, len_ref, q_hbm, k_hbm, v_hbm, out_ref,
+    q_ref, k_ref, v_ref, load, qp, kp, vp, r16, r8, r4, bias0, acc_s, peak_s,
     send16, recv16, send8, recv8, send4, recv4, fwd16, fwd8,
 ):
+    loads = [
+        pltpu.make_async_copy(src, dst, load.at[i])
+        for i, (src, dst) in enumerate(((k_hbm, k_ref), (v_hbm, v_ref), (q_hbm, q_ref)))
+    ]
+    for c in loads:
+        c.start()
     shard = q_ref.shape[0]
     segs = shard // SEG0
     chips = n // 2
@@ -109,7 +115,9 @@
             return 0
         lax.fori_loop(0, WIDTH // 256, column, 0)
 
+    loads[0].wait()
     permute(k_ref, kp)
+    loads[1].wait()
     permute(v_ref, vp)
 
     lane = iota((1, LANES), 1)
@@ -141,16 +149,21 @@
             device_id={"seq": peer}, device_id_type=MESH,
         )
 
-    first = []
-    for step in range(chips - 1, 0, -1):
-        first.append(copy(r16, me, send16.at[step], recv16, (chip + step) % chips * 2 + core))
-    first.append(copy(r8, me % 4, send8.at[1], recv8, mate))
-    first.append(copy(r16, me, send16.at[0], recv16, sibling))
-    first.append(copy(r8, me % 4, send8.at[0], recv8, sibling))
-    first.append(copy(r4, me % 2, send4.at[0], recv4, sibling))
+    turn = chip % 2
+    first = [
+        copy(r8, me % 4, send8.at[1], recv8, mate),
+        copy(r16, me, send16.at[chips], recv16, mate),
+        copy(r16, me, send16.at[0], recv16, sibling),
+        copy(r8, me % 4, send8.at[0], recv8, sibling),
+        copy(r4, me % 2, send4.at[0], recv4, sibling),
+    ]
+    others = [(mate_chip + (1 - 2 * turn) * step + chips) % chips for step in range(1, chips - 1)]
+    for step, other_chip in enumerate(others):
+        first.append(copy(r16, me, send16.at[step + 1], recv16, other_chip * 2 + core))
     for c in first:
         c.start()
 
+    loads[2].wait()
     permute(q_ref, qp)
 
     def bias_rows(place):
@@ -236,18 +249,6 @@
 
     lax.fori_loop(0, PAIRS // 2, near_step, 0)
 
-    second = []
-    for step in range(1, chips):
-        source = (chip + chips - step) % chips * 2 + core
-        copy(r16, source, send16.at[step], recv16, sibling).wait_recv()
-        c = copy(r16, source, fwd16.at[step], recv16, sibling)
-        c.start()
-        second.append(c)
-    copy(r8, mate % 4, send8.at[1], recv8, sibling).wait_recv()
-    c = copy(r8, mate % 4, fwd8.at[0], recv8, sibling)
-    c.start()
-    second.append(c)
-
     copy(r16, sibling, send16.at[0], recv16, sibling).wait_recv()
     copy(r8, sibling % 4, send8.at[0], recv8, sibling).wait_recv()
     copy(r4, sibling % 2, send4.at[0], recv4, sibling).wait_recv()
@@ -351,13 +352,30 @@
 
     lax.fori_loop(0, PAIRS // 2, functools.partial(far_step, (4,)), 0)
 
-    for step in range(1, chips):
-        source = (chip + chips - step) % chips * 2 + 1 - core
-        copy(r16, source, fwd16.at[step], recv16, sibling).wait_recv()
+    def forward(buf, slot, arrived, sent, recv):
+        copy(buf, slot, arrived, recv, sibling).wait_recv()
+        c = copy(buf, slot, sent, recv, sibling)
+        c.start()
+        return c
+
+    second = [
+        forward(r8, mate % 4, send8.at[1], fwd8.at[0], recv8),
+        forward(r16, mate, send16.at[chips], fwd16.at[0], recv16),
+    ]
+    for step, other_chip in enumerate(others):
+        second.append(
+            forward(r16, other_chip * 2 + core, send16.at[step + 1], fwd16.at[step + 1], recv16)
+        )
+
     far_mate = mate_chip * 2 + 1 - core
     copy(r8, far_mate % 4, fwd8.at[0], recv8, sibling).wait_recv()
-
-    lax.fori_loop(0, PAIRS // 2, functools.partial(far_step, (8, 16)), 0)
+    copy(r16, far_mate, fwd16.at[0], recv16, sibling).wait_recv()
+    lax.fori_loop(0, PAIRS // 2, functools.partial(far_step, (8,)), 0)
+
+    for step, other_chip in enumerate(others):
+        source = other_chip * 2 + 1 - core
+        copy(r16, source, fwd16.at[step + 1], recv16, sibling).wait_recv()
+    lax.fori_loop(0, PAIRS // 2, functools.partial(far_step, (16,)), 0)
 
     for c in first + second:
         c.wait_send()
@@ -384,10 +402,14 @@
     dma = pltpu.SemaphoreType.DMA
     shuffled = pl.pallas_call(
         functools.partial(kernel, n),
-        out_shape=jax.ShapeDtypeStruct((shard, WIDTH), BF16),
-        in_specs=[pl.BlockSpec(memory_space=pltpu.SMEM), vmem, vmem, vmem],
+        out_shape=pltpu.VMEM((shard, WIDTH), BF16),
+        in_specs=[pl.BlockSpec(memory_space=pltpu.SMEM)] + [pl.BlockSpec(memory_space=pl.ANY)] * 3,
         out_specs=vmem,
         scratch_shapes=[
+            pltpu.VMEM((shard, WIDTH), BF16),
+            pltpu.VMEM((shard, WIDTH), BF16),
+            pltpu.VMEM((shard, WIDTH), BF16),
+            dma((3,)),
             pltpu.VMEM((segs, SEG0, WIDTH), BF16),
             pltpu.VMEM((segs, SEG0, WIDTH), BF16),
             pltpu.VMEM((segs, SEG0, WIDTH), BF16),
@@ -397,7 +419,7 @@
             pltpu.VMEM((segs, LANES // 2, SEG0), BF16),
             pltpu.VMEM((HEADS, segs, SEG0, LANES), F32),
             pltpu.VMEM((HEADS, segs, SEG0 // 2, LANES), F32),
-            dma((chips,)), dma((n,)), dma((2,)), dma((4,)), dma((1,)), dma((2,)),
+            dma((chips + 1,)), dma((n,)), dma((2,)), dma((4,)), dma((1,)), dma((2,)),
             dma((chips,)), dma((1,)),
         ],
         compiler_params=pltpu.CompilerParams(

time: 39.8 us -> 37.7 us (0.947)
  Pallas kernels: 38.9 us -> 35.7 us
  local copies, waits for them, and re-layouts: 0 us -> 1.15 us
    pallas_call x1, Pallas kernels: 34.9 us -> 31.6 us  [per_device(): pl.pallas_call(functools.partial(kernel, n), out_shape=pltpu.VMEM((shard,...]
    unnamed x0 -> x2, local copies, waits for them, and re-layouts: none -> 1.15 us
where the time goes in v6:
time: 37.7 us; the launch traced here: 37.5 us
  Pallas kernels  35.7 us (95%)
  local copies, waits for them, and re-layouts  1.15 us (3%)
  between operations  0.67 us (2%)
    pallas_call x1, Pallas kernels, per_device(): pl.pallas_call(functools.partial(kernel, n), out_shape=pltpu.VMEM((shard,...  31.6 us
    pallas_call x1, Pallas kernels, per_device(): pl.pallas_call(restore, grid=(shard // (SEG0 // 2),), out_shape=jax.Shape...  4.05 us
    unnamed x2, local copies, waits for them, and re-layouts  1.15 us

profile of v6, /device:TPU:0, one launch (start us, length us, event | category | flops | bytes accessed | tf_op | source)
XLA Modules:
  0.0 37.5 jit_solution(17383048736040951031)
XLA Ops:
  0.7 31.6 %shard_map.46.rows_ref = bf16[1024,768]{1,0:T(8,128)(2,1)S(1)} custom-call(s32[1]{0:T(128)S(6)} %copy.5.len_ref, bf16[1024,768]{1,0:T(8,128)(2,1)} %q_hbm.1, bf16[1024,768]{1,0:T(8,128)(2,1)} %k_hbm.1, bf16[1024,768]{1,0:T(8,128)(2,1)} %v_hbm.1), custom_call_target="tpu_custom_call" | custom-call | flops 3221225472 | bytes 6291456 | tf_op jit(solution)/shard_map/pallas_call | solution.py:403
  32.3 0.0 copy-start
  32.3 1.1 %copy-done = bf16[1024,768]{1,0:T(8,128)(2,1)} copy-done((bf16[1024,768]{1,0:T(8,128)(2,1)}, bf16[1024,768]{1,0:T(8,128)(2,1)S(1)}, u32[]{:S(2)}) %copy-start) | copy-done | bytes 1572888
  33.4 4.0 %shard_map.47 = bf16[1024,768]{1,0:T(8,128)(2,1)} custom-call(s32[1]{0:T(128)S(6)} %copy.5.len_ref, bf16[1024,768]{1,0:T(8,128)(2,1)} %copy-done), custom_call_target="tpu_custom_call" | custom-call | tf_op jit(solution)/shard_map/pallas_call | solution.py:434
Async XLA Ops:
  32.3 1.2 %copy-start = (bf16[1024,768]{1,0:T(8,128)(2,1)}, bf16[1024,768]{1,0:T(8,128)(2,1)S(1)}, u32[]{:S(2)}) copy-start(bf16[1024,768]{1,0:T(8,128)(2,1)S(1)} %shard_map.46.rows_ref) | copy-start | bytes 4718596

commit v7 on v6

--- a/solution.py
+++ b/solution.py
@@ -382,14 +382,15 @@
 
 
 def restore(len_ref, rows_ref, out_ref):
-    half, width = rows_ref.shape
+    half, width = out_ref.shape
     sub = half // CLASSES
     new = iota((half, half), 0)
     old = iota((half, half), 1)
     back = jnp.where(new == ((old & (sub - 1)) << 4) + bitrev(old >> 4), 1.0, 0.0).astype(BF16)
     first = (lax.axis_index("seq") * pl.num_programs(0) + pl.program_id(0)) * half
     valid = first + iota((half, 1), 0) < len_ref[0]
-    moved = jnp.dot(back, rows_ref[...], preferred_element_type=F32)
+    rows = rows_ref[pl.ds(pl.multiple_of(pl.program_id(0) * half, half), half), :]
+    moved = dot(back, rows)
     out_ref[...] = jnp.where(valid, moved, 0.0).astype(BF16)
 
 
@@ -423,7 +424,7 @@
             dma((chips,)), dma((1,)),
         ],
         compiler_params=pltpu.CompilerParams(
-            collective_id=0, has_side_effects=True, vmem_limit_bytes=56 * 1024 * 1024
+            collective_id=0, has_side_effects=True, vmem_limit_bytes=52 * 1024 * 1024
         ),
         cost_estimate=pl.CostEstimate(
             flops=256 * shard * HEADS * 1024, bytes_accessed=8 * shard * WIDTH,
@@ -435,9 +436,10 @@
         restore,
         grid=(shard // (SEG0 // 2),),
         out_shape=jax.ShapeDtypeStruct((shard, WIDTH), BF16),
-        in_specs=[pl.BlockSpec(memory_space=pltpu.SMEM), block],
+        in_specs=[pl.BlockSpec(memory_space=pltpu.SMEM), vmem],
         out_specs=block,
-    )(slide_length, shuffled)
+        compiler_params=pltpu.CompilerParams(vmem_limit_bytes=16 * 1024 * 1024),
+    )(slide_length, pltpu.with_memory_space_constraint(shuffled, pltpu.VMEM))
 
 
 def solution(mesh):

time: 37.7 us -> 34.8 us (0.923)
  Pallas kernels: 35.7 us -> 34 us
  local copies, waits for them, and re-layouts: 1.15 us -> 0 us
    pallas_call x1, Pallas kernels: 4.05 us -> 2.34 us  [per_device(): pl.pallas_call(restore, grid=(shard // (SEG0 // 2),), out_shape=jax.Shape...]
    unnamed x2 -> x0, local copies, waits for them, and re-layouts: 1.15 us -> none
where the time goes in v7:
time: 34.8 us; the launch traced here: 34.6 us
  Pallas kernels  34 us (98%)
  between operations  0.66 us (2%)
    pallas_call x1, Pallas kernels, per_device(): pl.pallas_call(functools.partial(kernel, n), out_shape=pltpu.VMEM((shard,...  31.6 us
    pallas_call x1, Pallas kernels, per_device(): pl.pallas_call(restore, grid=(shard // (SEG0 // 2),), out_shape=jax.Shape...  2.34 us

profile of v7, /device:TPU:0, one launch (start us, length us, event | category | flops | bytes accessed | tf_op | source)
XLA Modules:
  0.0 34.6 jit_solution(6929088168446694680)
XLA Ops:
  0.7 31.6 %shard_map.46.rows_ref = bf16[1024,768]{1,0:T(8,128)(2,1)S(1)} custom-call(s32[1]{0:T(128)S(6)} %copy.5.len_ref, bf16[1024,768]{1,0:T(8,128)(2,1)} %q_hbm.1, bf16[1024,768]{1,0:T(8,128)(2,1)} %k_hbm.1, bf16[1024,768]{1,0:T(8,128)(2,1)} %v_hbm.1), custom_call_target="tpu_custom_call" | custom-call | flops 3221225472 | bytes 6291456 | tf_op jit(solution)/shard_map/pallas_call | solution.py:404
  32.3 2.3 %shard_map.47 = bf16[1024,768]{1,0:T(8,128)(2,1)} custom-call(s32[1]{0:T(128)S(6)} %copy.5.len_ref, bf16[1024,768]{1,0:T(8,128)(2,1)S(1)} %shard_map.46.rows_ref), custom_call_target="tpu_custom_call" | custom-call | tf_op jit(solution)/shard_map/pallas_call | solution.py:435
